TPU v7x, 32 devices: a whole 2x2x4 slice. The times are simulated.
32 devices in a mesh: row: 4 (over z), col: 4 (over x, core), depth: 2 (over y).
Axes of the slice: x: 2, y: 2, z: 4, core: 2. Of those that a mesh axis runs over, the one named last changes fastest.
Arguments:
- intersection_re: bfloat16 [2, 4096, 4096], P('depth', ('row', 'col')), may hold values from -1 to 1, as said below
- intersection_im: bfloat16 [2, 4096, 4096], P('depth', ('row', 'col')), may hold values from -1 to 1, as said below
- weights: float32 [2], replicated, may hold values from 0.5 to 2
- shells: int32 [2, 3], replicated, may hold values from -2 to 2
- rotation: bfloat16 [4096, 4096], P(('row', 'col')), may hold values from -6 to 6
Outputs:
- updated: float32 [4096, 4096], P(('row', 'col'), 'depth')
Inputs may be any that keep to these rules, and one draw needn't show every extreme that they name: `intersection_re`: diagonal entries lie in 0.5 to 1. `intersection_im`: diagonal entries lie in -0.6 to 0.6.
All inputs are finite; a program needn't handle non-finite values.
Results may differ from a plain program's by a relative error of at most 0.035.
Values may be sent and summed in bfloat16 or wider, within the bound.
A program may use at most 64 MiB of HBM per device.

v0:
```python
import math

import jax
import jax.numpy as jnp
from jax import lax
from jax.sharding import PartitionSpec as P

TERMS = 8


LATTICE = 0.25


def per_device(intersection_re, intersection_im, weights, shells, rotation):
    shells_here = intersection_re.shape[0]
    slab_rows = intersection_re.shape[1]
    width = intersection_re.shape[2]
    position = lax.axis_index(("row", "col"))
    layer_index = lax.axis_index("depth")
    depth_count = lax.axis_size("depth")
    block_re = lax.dynamic_slice_in_dim(intersection_re, position * slab_rows, slab_rows, 2)
    block_im = lax.dynamic_slice_in_dim(intersection_im, position * slab_rows, slab_rows, 2)
    diag_piece = jnp.stack(
        [jnp.diagonal(block_re, axis1=1, axis2=2), jnp.diagonal(block_im, axis1=1, axis2=2)], 1
    )
    first_shell = layer_index * shells_here
    own_weights = lax.dynamic_slice_in_dim(weights, first_shell, shells_here, 0)
    own_vectors = (
        lax.dynamic_slice_in_dim(shells, first_shell, shells_here, 0).astype(jnp.float32) * LATTICE
    )
    diagonals = lax.all_gather(diag_piece, ("row", "col"), axis=2, tiled=True).astype(jnp.float32)
    diag_re = diagonals[:, 0]
    diag_im = diagonals[:, 1]
    phase_own = jnp.arctan2(diag_im, diag_re)
    partial_centre = -jnp.einsum("bk,bn->kn", own_weights[:, None] * own_vectors, phase_own)
    centre = lax.psum(partial_centre, "depth")
    spread = phase_own + jnp.einsum("bk,kn->bn", own_vectors, centre)
    modulus = diag_re * diag_re + diag_im * diag_im
    values_re = intersection_re.astype(jnp.float32)
    values_im = intersection_im.astype(jnp.float32)
    terms = values_re * diag_re[:, None, :] + values_im * diag_im[:, None, :]
    terms = (
        terms
        - spread[:, None, :]
        * (values_im * diag_re[:, None, :] - values_re * diag_im[:, None, :])
        / modulus[:, None, :]
    )
    local_sum = jnp.sum(own_weights[:, None, None] * terms, 0)
    factor = 1.25 / math.sqrt(depth_count * shells_here)
    slab_cols = width // depth_count
    mirrored = lax.all_to_all(local_sum, ("row", "col"), split_axis=1, concat_axis=0, tiled=True).T
    operator_rows = (
        lax.psum_scatter(local_sum - mirrored, "depth", scatter_dimension=1, tiled=True) * factor
    )
    operator_piece = operator_rows.astype(jnp.bfloat16)
    operator_cols = lax.all_gather(operator_piece, ("row", "col"), axis=0, tiled=True)
    accum = lax.dynamic_slice_in_dim(rotation, layer_index * slab_cols, slab_cols, 1).astype(
        jnp.float32
    )
    product = jnp.dot(rotation, operator_cols, preferred_element_type=jnp.float32)
    for order in range(1, TERMS):
        series_term = (product / order).astype(jnp.bfloat16)
        accum = accum + series_term.astype(jnp.float32)
        if order + 1 < TERMS:
            piece = lax.all_gather(series_term, "depth", axis=1, tiled=True)
            matching = lax.slice_in_dim(operator_cols, 0, piece.shape[1], axis=0)
            product = jnp.zeros_like(accum) + jnp.dot(
                piece, matching, preferred_element_type=jnp.float32
            )
    return accum


def solution(mesh):
    in_specs = (
        P("depth", ("row", "col"), None),
        P("depth", ("row", "col"), None),
        P(),
        P(),
        P(("row", "col"), None),
    )
    out_specs = P(("row", "col"), "depth")
    return jax.shard_map(
        per_device, mesh=mesh, in_specs=in_specs, out_specs=out_specs, check_vma=False
    )
```

profile of v0, /device:TPU:0, one launch (start us, length us, event | category | flops | bytes accessed | tf_op | source)
XLA Modules:
  0.0 647.5 jit_solution(8676654230727425514)
XLA Ops:
  6.6 1.1 dynamic-slice_bitcast_fusion
  7.7 2.5 gather_fusion.1
  10.2 2.5 gather_fusion
  12.7 23.1 %all_gather.24 = bf16[1,2,4096]{2,1,0:T(2,128)(2,1)S(1)} all-gather(bf16[1,2,256]{2,1,0:T(2,128)(2,1)S(1)} %pad_maximum_fusion), channel_id=1, replica_groups=mesh['row'=4,'col'=4,'depth'=2] {'row','col'}, dimensions={2}, use_global_device_ids=true | all-gather | bytes 17408 | tf_op jit(solution)/shard_map/all_gather | solution.py:31
  35.9 4.1 copy.34
  39.9 4.1 copy.35
  44.0 0.2 slice_atan2_fusion
  44.3 0.6 dynamic_slice.16
  45.6 0.1 multiply_negate_fusion
  45.7 8.9 %psum.7 = bf16[3,4096]{1,0:T(4,128)(2,1)S(1)} all-reduce(f32[3,4096]{1,0:T(4,128)S(1)} %multiply_negate_fusion), channel_id=1, replica_groups=mesh['row'=4,'col'=4,'depth'=2] {'depth'}, use_global_device_ids=true, to_apply=%region_0.1 | all-reduce | flops 12288 | bytes 73728 | tf_op jit(solution)/shard_map/psum | solution.py:36
  54.6 0.1 fusion.16
  54.8 8.2 %fusion.2 = f32[1,256,4096]{1,2,0:T(8,128)} fusion(bf16[1,256,4096]{1,2,0:T(8,128)(2,1)} %copy.34, bf16[1,256,4096]{1,2,0:T(8,128)(2,1)} %copy.35, f32[4096]{0:T(1024)S(1)} %bitcast.50, f32[4096]{0:T(1024)S(1)} %atan2_add_fusion, f32[4096]{0:T(1024)S(1)} %bitcast.49, f32[4096]{0:T(1024)S(1)} %bitcast.47, f32[]{:T(128)} %bitcast), kind=kLoop, calls=%fused_computation.8 | loop fusion | flops 12582912 | bytes 8454148 | tf_op jit(solution)/shard_map/mul | solution.py:48
  63.0 5.4 copy.36
  68.5 96.2 %all_to_all.19 = f32[256,16,256]{2,0,1:T(8,128)S(1)} all-to-all(f32[256,16,256]{2,0,1:T(8,128)} %copy.36), channel_id=1, replica_groups=mesh['row'=4,'col'=4,'depth'=2] {'row','col'}, dimensions={1} | all-to-all | bytes 8388608 | tf_op jit(solution)/shard_map/all_to_all | solution.py:51
  164.7 2.8 bitcast_subtract_fusion
  167.4 0.0 reduce-scatter.2.cloned.1.call-update
  167.4 0.0 all-gather.8.cloned.1.call-start
  167.5 53.8 %reduce-scatter.2.cloned.1.call-done = f32[256,2048]{0,1:T(8,128)} async-done(((f32[256,4096]{0,1:T(8,128)}), f32[256,2048]{0,1:T(8,128)}) %reduce-scatter.2.cloned.1.call-update) | async-done | bytes 2097168 | tf_op jit(solution)/shard_map/reduce_scatter | solution.py:53
  221.3 2.8 multiply_convert_fusion
  224.1 0.0 all-gather.8.cloned.1.call-update
  224.1 0.0 all-gather.10.cloned.1.call-start
  224.1 130.4 %all-gather.8.cloned.1.call-done = bf16[4096,2048]{0,1:T(8,128)(2,1)} async-done(((bf16[256,2048]{0,1:T(8,128)(2,1)}), bf16[4096,2048]{0,1:T(8,128)(2,1)}) %all-gather.8.cloned.1.call-update) | async-done | bytes 16777232 | tf_op jit(solution)/shard_map/all_gather | solution.py:56
  354.6 9.3 %fusion.14 = bf16[256,2048]{0,1:T(8,128)(2,1)} fusion(bf16[4096,2048]{0,1:T(8,128)(2,1)} %all-gather.8.cloned.1.call-done, bf16[256,4096]{1,0:T(8,128)(2,1)S(1)} %copy-done), kind=kOutput, calls=%fused_computation.28 | convolution fusion | flops 4295491584 | bytes 19922944 | tf_op jit(solution)/shard_map/dot_general | solution.py:60
  363.8 0.0 all-gather.10.cloned.1.call-update
  363.8 0.0 all-gather.12.cloned.1.call-start
  363.9 31.4 %all-gather.10.cloned.1.call-done = bf16[256,4096]{0,1:T(8,128)(2,1)} async-done(((bf16[256,2048]{0,1:T(8,128)(2,1)}), bf16[256,4096]{0,1:T(8,128)(2,1)}) %all-gather.10.cloned.1.call-update) | async-done | bytes 2097168 | tf_op jit(solution)/shard_map/all_gather | solution.py:65
  395.3 12.0 %fusion.6 = bf16[256,2048]{0,1:T(8,128)(2,1)} fusion(bf16[4096,2048]{0,1:T(8,128)(2,1)} %all-gather.8.cloned.1.call-done, bf16[256,4096]{0,1:T(8,128)(2,1)} %all-gather.10.cloned.1.call-done), kind=kOutput, calls=%fused_computation.19 | convolution fusion | flops 4296015872 | bytes 19922944 | tf_op jit(solution)/shard_map/dot_general | solution.py:67
  407.3 0.0 all-gather.12.cloned.1.call-update
  407.4 9.7 %all-gather.14.cloned.1.call-start = ((), (), s32[]{:S(2)}) async-start(), calls=%async_computation.6 | async-start | bytes 3145728 | tf_op jit(solution)/shard_map/all_gather | solution.py:65
  417.1 23.6 %all-gather.12.cloned.1.call-done = bf16[256,4096]{0,1:T(8,128)(2,1)} async-done(((bf16[256,2048]{0,1:T(8,128)(2,1)}), bf16[256,4096]{0,1:T(8,128)(2,1)}) %all-gather.12.cloned.1.call-update) | async-done | bytes 2097168 | tf_op jit(solution)/shard_map/all_gather | solution.py:65
  440.6 12.0 %fusion.7 = bf16[256,2048]{0,1:T(8,128)(2,1)} fusion(bf16[4096,2048]{0,1:T(8,128)(2,1)} %all-gather.8.cloned.1.call-done, bf16[256,4096]{0,1:T(8,128)(2,1)} %all-gather.12.cloned.1.call-done), kind=kOutput, calls=%fused_computation.20 | convolution fusion | flops 4296015872 | bytes 19922944 | tf_op jit(solution)/shard_map/dot_general | solution.py:67
  452.7 0.0 all-gather.16.cloned.1.call-start
  452.7 33.2 %all-gather.14.cloned.1.call-done = bf16[256,4096]{0,1:T(8,128)(2,1)} async-done(((bf16[256,2048]{0,1:T(8,128)(2,1)}), bf16[256,4096]{0,1:T(8,128)(2,1)}) %all-gather.14.cloned.1.call-update) | async-done | bytes 2097168 | tf_op jit(solution)/shard_map/all_gather | solution.py:65
  486.0 12.0 %fusion.8 = bf16[256,2048]{0,1:T(8,128)(2,1)} fusion(bf16[4096,2048]{0,1:T(8,128)(2,1)} %all-gather.8.cloned.1.call-done, bf16[256,4096]{0,1:T(8,128)(2,1)} %all-gather.14.cloned.1.call-done), kind=kOutput, calls=%fused_computation.21 | convolution fusion | flops 4296015872 | bytes 19922944 | tf_op jit(solution)/shard_map/dot_general | solution.py:67
  497.9 0.0 all-gather.16.cloned.1.call-update
  498.0 0.0 all-gather.18.cloned.1.call-start
  498.0 33.2 %all-gather.16.cloned.1.call-done = bf16[256,4096]{0,1:T(8,128)(2,1)} async-done(((bf16[256,2048]{0,1:T(8,128)(2,1)}), bf16[256,4096]{0,1:T(8,128)(2,1)}) %all-gather.16.cloned.1.call-update) | async-done | bytes 2097168 | tf_op jit(solution)/shard_map/all_gather | solution.py:65
  531.2 12.1 %fusion.9 = bf16[256,2048]{0,1:T(8,128)(2,1)} fusion(bf16[4096,2048]{0,1:T(8,128)(2,1)} %all-gather.8.cloned.1.call-done, bf16[256,4096]{0,1:T(8,128)(2,1)} %all-gather.16.cloned.1.call-done), kind=kOutput, calls=%fused_computation.22 | convolution fusion | flops 4296015872 | bytes 19922944 | tf_op jit(solution)/shard_map/dot_general | solution.py:67
  543.4 0.0 all-gather.18.cloned.1.call-update
  543.4 0.2 all-gather.20.cloned.1.call-start
  543.6 33.0 %all-gather.18.cloned.1.call-done = bf16[256,4096]{0,1:T(8,128)(2,1)} async-done(((bf16[256,2048]{0,1:T(8,128)(2,1)}), bf16[256,4096]{0,1:T(8,128)(2,1)}) %all-gather.18.cloned.1.call-update) | async-done | bytes 2097168 | tf_op jit(solution)/shard_map/all_gather | solution.py:65
  576.7 12.1 %fusion.10 = bf16[256,2048]{0,1:T(8,128)(2,1)} fusion(bf16[4096,2048]{0,1:T(8,128)(2,1)} %all-gather.8.cloned.1.call-done, bf16[256,4096]{0,1:T(8,128)(2,1)} %all-gather.18.cloned.1.call-done), kind=kOutput, calls=%fused_computation.23 | convolution fusion | flops 4296015872 | bytes 19922944 | tf_op jit(solution)/shard_map/dot_general | solution.py:67
  588.8 0.0 all-gather.20.cloned.1.call-update
  588.8 0.1 constant_dynamic-slice_fusion.1
  588.9 1.3 copy.50
  590.2 31.9 %all-gather.20.cloned.1.call-done = bf16[256,4096]{0,1:T(8,128)(2,1)} async-done(((bf16[256,2048]{0,1:T(8,128)(2,1)}), bf16[256,4096]{0,1:T(8,128)(2,1)}) %all-gather.20.cloned.1.call-update) | async-done | bytes 2097168 | tf_op jit(solution)/shard_map/all_gather | solution.py:65
  622.1 15.3 %fusion.13 = f32[256,2048]{0,1:T(8,128)} fusion(bf16[4096,2048]{0,1:T(8,128)(2,1)} %all-gather.8.cloned.1.call-done, bf16[256,4096]{0,1:T(8,128)(2,1)} %all-gather.20.cloned.1.call-done, bf16[256,2048]{0,1:T(8,128)(2,1)} %fusion.10, bf16[256,2048]{0,1:T(8,128)(2,1)} %fusion.9, bf16[256,2048]{0,1:T(8,128)(2,1)} %fusion.8, bf16[256,2048]{0,1:T(8,128)(2,1)} %fusion.7, ...), kind=kOutput, calls=%fused_computation.27 | convolution fusion | flops 4303880192 | bytes 28311552 | tf_op jit(solution)/shard_map/dot_general | solution.py:67
  637.4 2.9 copy.43
  (18 shorter events, 0.2 us)
Async XLA Ops:
  6.5 348.0 %copy-start = (bf16[256,4096]{1,0:T(8,128)(2,1)S(1)}, bf16[256,4096]{1,0:T(8,128)(2,1)}, u32[]{:S(2)}) copy-start(bf16[256,4096]{1,0:T(8,128)(2,1)} %param.9) | copy-start | bytes 6291460
  6.5 214.8 %reduce-scatter.2.cloned.1.call-start = ((), (), s32[]{:S(2)}) async-start(), calls=%async_computation.2 | async-start | bytes 6291456 | tf_op jit(solution)/shard_map/reduce_scatter | solution.py:53
  39.9 4.3 copy-start.3
  39.9 5.6 copy-start.2
  68.5 96.2 %copy-start.1 = (f32[1,256,4096]{1,2,0:T(8,128)S(1)}, f32[1,256,4096]{1,2,0:T(8,128)}, u32[]{:S(2)}) copy-start(f32[1,256,4096]{1,2,0:T(8,128)} %fusion.2) | copy-start | bytes 12582916
  167.4 187.1 %all-gather.8.cloned.1.call-start = ((), (), s32[]{:S(2)}) async-start(), calls=%async_computation.3 | async-start | bytes 17825792 | tf_op jit(solution)/shard_map/all_gather | solution.py:56
  224.1 171.2 %all-gather.10.cloned.1.call-start = ((), (), s32[]{:S(2)}) async-start(), calls=%async_computation.4 | async-start | bytes 3145728 | tf_op jit(solution)/shard_map/all_gather | solution.py:65
  363.8 76.8 %all-gather.12.cloned.1.call-start = ((), (), s32[]{:S(2)}) async-start(), calls=%async_computation.5 | async-start | bytes 3145728 | tf_op jit(solution)/shard_map/all_gather | solution.py:65
  407.4 78.6 %all-gather.14.cloned.1.call-start = ((), (), s32[]{:S(2)}) async-start(), calls=%async_computation.6 | async-start | bytes 3145728 | tf_op jit(solution)/shard_map/all_gather | solution.py:65
  452.7 78.6 %all-gather.16.cloned.1.call-start = ((), (), s32[]{:S(2)}) async-start(), calls=%async_computation.7 | async-start | bytes 3145728 | tf_op jit(solution)/shard_map/all_gather | solution.py:65
  498.0 78.7 %all-gather.18.cloned.1.call-start = ((), (), s32[]{:S(2)}) async-start(), calls=%async_computation.8 | async-start | bytes 3145728 | tf_op jit(solution)/shard_map/all_gather | solution.py:65
  543.4 78.7 %all-gather.20.cloned.1.call-start = ((), (), s32[]{:S(2)}) async-start(), calls=%async_computation.9 | async-start | bytes 3145728 | tf_op jit(solution)/shard_map/all_gather | solution.py:65
Sparse Core Ops, SparseCore 0:
  167.6 53.6 reduce-scatter.1
  224.2 130.3 all-gather.7
  364.0 31.2 all-gather.9
  407.5 33.1 all-gather.11
  452.8 33.1 all-gather.13
  498.1 33.1 all-gather.15
  543.5 33.1 all-gather.17
  588.9 33.1 all-gather.19
where the time goes:
time: 656 us; the launch traced here: 647 us
  waiting for transfers between devices  371 us (57%)
  blocking collectives  128 us (20%)
  matrix products  85 us (13%)
  local copies, waits for them, and re-layouts  24.7 us (4%)
  between operations  14.6 us (2%)
  other arithmetic  14.2 us (2%)
  starting transfers between devices  10.1 us (2%)
    all_gather x6, waiting for transfers between devices, per_device(): piece = lax.all_gather(series_term, 'depth', axis=1, tiled=True)  186 us
    all_gather x1, waiting for transfers between devices, per_device(): lax.all_gather(operator_piece, ('row', 'col'), axis=0, tiled=True)  130 us
    all_to_all x1, blocking collectives, per_device(): lax.all_to_all(local_sum, ('row', 'col'), split_axis=1, concat_axis=0, ti...  96.2 us
    dot_general x6, matrix products, per_device(): jnp.dot(piece, matching, preferred_element_type=jnp.float32)  75.6 us
    reduce_scatter x1, waiting for transfers between devices, per_device(): lax.psum_scatter(local_sum - mirrored, 'depth', scatter_dimension=1, tile...  53.8 us
    all_gather x1, blocking collectives, per_device(): lax.all_gather(diag_piece, ('row', 'col'), axis=2, tiled=True)  23.1 us
  transfers between devices with their start and end apart: 8, of which 8 were waited for; matrix products, arithmetic and copies ran while one was open for 0% of the time, Pallas kernels for 0%

commit v1 on v0

--- a/solution.py
+++ b/solution.py
@@ -1,8 +1,11 @@
+import functools
 import math
 
 import jax
 import jax.numpy as jnp
 from jax import lax
+from jax.experimental import pallas as pl
+from jax.experimental.pallas import tpu as pltpu
 from jax.sharding import PartitionSpec as P
 
 TERMS = 8
@@ -11,7 +14,215 @@
 LATTICE = 0.25
 
 
-def per_device(intersection_re, intersection_im, weights, shells, rotation):
+def shift(at, axis, way):
+    z, x, y, core = at
+    if axis == "z":
+        return (z + way, x, y, core)
+    if axis == "x":
+        return (z, 1 - x, y, core)
+    if axis == "y":
+        return (z, x, 1 - y, core)
+    return (z, x, y, 1 - core)
+
+
+def device_of(at):
+    z, x, y, core = at
+    return {"row": z, "col": x * 2 + core, "depth": y}
+
+
+ORDERS = (("z", "x", "y"), ("x", "y", "z"), ("y", "z", "x"))
+
+
+def cut(width, parts):
+    unit = width // 128
+    ends = [unit * i // parts * 128 for i in range(parts + 1)]
+    return [(ends[i], ends[i + 1] - ends[i]) for i in range(parts)]
+
+
+def series_kernel(
+    rows_count, piece_ref, rotation_ref, out_ref,
+    gen, term, accum, sent, got,
+    own_sem, link_sem, side_sem, send_sem, last_send, last_recv,
+):
+    z = lax.axis_index("row")
+    col = lax.axis_index("col")
+    y = lax.axis_index("depth")
+    x = col // 2
+    core = col % 2
+    me = (z, x, y, core)
+    rows, width = piece_ref.shape
+    segments = cut(width, len(ORDERS))
+
+    def exists(axis, way):
+        if axis != "z":
+            return None
+        return z > 0 if way < 0 else z < rows_count - 1
+
+    def guarded(condition, action):
+        if condition is None:
+            action()
+        else:
+            pl.when(condition)(action)
+
+    barrier = pltpu.get_barrier_semaphore()
+    moves = [("z", -1), ("z", 1), ("x", 1), ("y", 1), ("core", 1)]
+    for axis, way in moves:
+        def greet(axis=axis, way=way):
+            pl.semaphore_signal(
+                barrier, inc=1, device_id=device_of(shift(me, axis, way)),
+                device_id_type=pl.DeviceIdType.MESH,
+            )
+        guarded(exists(axis, way), greet)
+    peers = 3 + jnp.where(z > 0, 1, 0) + jnp.where(z < rows_count - 1, 1, 0)
+    pl.semaphore_wait(barrier, peers)
+
+    def slab(at):
+        zo, xo, yo, co = at
+        return ((zo * 2 + xo) * 2 + co) * 2 + yo
+
+    own = pltpu.make_async_copy(
+        piece_ref, gen.at[pl.ds(pl.multiple_of(slab(me) * rows, rows), rows), :], own_sem
+    )
+    own.start()
+    own.wait()
+
+    def copy(seg, origin, move, recv):
+        start, size = segments[seg]
+        place = gen.at[
+            pl.ds(pl.multiple_of(slab(origin) * rows, rows), rows), pl.ds(start, size)
+        ]
+        axis, way = move
+        return pltpu.make_async_remote_copy(
+            src_ref=place, dst_ref=place,
+            send_sem=send_sem.at[seg, moves.index(move), slab(origin) % (rows_count * 8)],
+            recv_sem=recv.at[seg, slab(origin)],
+            device_id=device_of(shift(me, axis, way)),
+            device_id_type=pl.DeviceIdType.MESH,
+        )
+
+    plan = []
+    for dz in range(1 - rows_count, rows_count):
+        for dx in range(2):
+            for dy in range(2):
+                for seg, order in enumerate(ORDERS):
+                    offset = {"z": dz, "x": dx, "y": dy}
+                    last = max([i for i, a in enumerate(order) if offset[a]], default=-1)
+                    onward = []
+                    if last >= 0 and order[last] == "z":
+                        onward.append(("z", 1 if dz < 0 else -1))
+                    for axis in order[last + 1:]:
+                        onward += [("z", -1), ("z", 1)] if axis == "z" else [(axis, 1)]
+                    plan.append((abs(dz) + dx + dy, seg, dz, dx, dy, onward))
+    plan.sort(key=lambda entry: entry[:2])
+
+    def origin_of(dz, dx, dy):
+        return (z + dz, 1 - x if dx else x, 1 - y if dy else y, core)
+
+    def inside(dz):
+        if dz == 0:
+            return None
+        return z + dz >= 0 if dz < 0 else z + dz < rows_count
+
+    for hops, seg, dz, dx, dy, onward in plan:
+        def handle(hops=hops, seg=seg, dz=dz, dx=dx, dy=dy, onward=onward):
+            origin = origin_of(dz, dx, dy)
+            if hops:
+                copy(seg, origin, ("x", 1), link_sem).wait_recv()
+            for move in onward:
+                guarded(exists(*move), lambda move=move: copy(seg, origin, move, link_sem).start())
+            copy(seg, origin, ("core", 1), side_sem).start()
+        guarded(inside(dz), handle)
+
+    for seg in range(len(ORDERS)):
+        for zo in range(rows_count):
+            for xo in range(2):
+                for yo in range(2):
+                    copy(seg, (zo, xo, yo, 1 - core), ("core", 1), side_sem).wait_recv()
+
+    chunk = 512
+    half = width // 2
+    other = device_of(shift(me, "y", 1))
+
+    def last_copy(index):
+        place = pl.ds(index * chunk, chunk)
+        return pltpu.make_async_remote_copy(
+            src_ref=sent.at[:, place], dst_ref=got.at[:, place],
+            send_sem=last_send.at[index], recv_sem=last_recv.at[index],
+            device_id=other, device_id_type=pl.DeviceIdType.MESH,
+        )
+
+    own_rows = pl.ds(pl.multiple_of(y * rows, rows), rows)
+    other_rows = pl.ds(pl.multiple_of((1 - y) * rows, rows), rows)
+    for order in range(1, TERMS):
+        source = rotation_ref if order == 1 else term.at[(order - 1) % 2]
+
+        def product(place):
+            value = jnp.dot(source[...], gen[:, place], preferred_element_type=jnp.float32)
+            return (value * (1.0 / order)).astype(jnp.bfloat16)
+
+        if order + 1 < TERMS:
+            @pl.loop(0, width // chunk)
+            def _(index):
+                place = pl.ds(pl.multiple_of(index * chunk, chunk), chunk)
+                value = product(place)
+                term[order % 2, :, place] = value
+                base = rotation_ref[:, place].astype(jnp.float32) if order == 1 else accum[:, place]
+                accum[:, place] = base + value.astype(jnp.float32)
+        else:
+            for index in range(half // chunk):
+                place = pl.ds(pl.multiple_of((1 - y) * half + index * chunk, chunk), chunk)
+                total = accum[:, place] + product(place).astype(jnp.float32)
+                sent[:, index * chunk:(index + 1) * chunk] = total.astype(jnp.bfloat16)
+                last_copy(index).start()
+            for index in range(half // chunk):
+                place = pl.ds(pl.multiple_of(y * half + index * chunk, chunk), chunk)
+                total = accum[:, place] + product(place).astype(jnp.float32)
+                out_ref[own_rows, index * chunk:(index + 1) * chunk] = total
+    for index in range(half // chunk):
+        last_copy(index).wait_recv()
+        part = slice(index * chunk, (index + 1) * chunk)
+        out_ref[other_rows, part] = got[:, part].astype(jnp.float32)
+    for index in range(half // chunk):
+        last_copy(index).wait_send()
+    for hops, seg, dz, dx, dy, onward in plan:
+        def finish(seg=seg, dz=dz, dx=dx, dy=dy, onward=onward):
+            origin = origin_of(dz, dx, dy)
+            for move in onward:
+                guarded(exists(*move), lambda move=move: copy(seg, origin, move, link_sem).wait_send())
+            copy(seg, origin, ("core", 1), side_sem).wait_send()
+        guarded(inside(dz), finish)
+
+
+def series(rows_count, piece, rotation_piece):
+    rows, width = piece.shape
+    pieces = rows_count * 8
+    segs = len(ORDERS)
+    vmem = pl.BlockSpec(memory_space=pltpu.VMEM)
+    return pl.pallas_call(
+        functools.partial(series_kernel, rows_count),
+        out_shape=jax.ShapeDtypeStruct((2 * rows, width // 2), jnp.float32),
+        in_specs=[vmem, vmem],
+        out_specs=vmem,
+        scratch_shapes=[
+            pltpu.VMEM((width, width), jnp.bfloat16),
+            pltpu.VMEM((2, rows, width), jnp.bfloat16),
+            pltpu.VMEM((rows, width), jnp.float32),
+            pltpu.VMEM((rows, width // 2), jnp.bfloat16),
+            pltpu.VMEM((rows, width // 2), jnp.bfloat16),
+            pltpu.SemaphoreType.DMA,
+            pltpu.SemaphoreType.DMA((segs, pieces)),
+            pltpu.SemaphoreType.DMA((segs, pieces)),
+            pltpu.SemaphoreType.DMA((segs, 5, pieces)),
+            pltpu.SemaphoreType.DMA((width // 1024,)),
+            pltpu.SemaphoreType.DMA((width // 1024,)),
+        ],
+        compiler_params=pltpu.CompilerParams(
+            collective_id=3, has_side_effects=True, vmem_limit_bytes=50 * 2**20
+        ),
+    )(piece, rotation_piece)
+
+
+def per_device(rows_count, fast, intersection_re, intersection_im, weights, shells, rotation):
     shells_here = intersection_re.shape[0]
     slab_rows = intersection_re.shape[1]
     width = intersection_re.shape[2]
@@ -48,6 +259,16 @@
     local_sum = jnp.sum(own_weights[:, None, None] * terms, 0)
     factor = 1.25 / math.sqrt(depth_count * shells_here)
     slab_cols = width // depth_count
+    if fast:
+        narrow = local_sum.astype(jnp.bfloat16)
+        mirrored = lax.all_to_all(narrow, ("row", "col"), split_axis=1, concat_axis=0, tiled=True)
+        anti = (local_sum - mirrored.T.astype(jnp.float32)) * factor
+        piece = lax.psum_scatter(
+            anti.astype(jnp.bfloat16), "depth", scatter_dimension=0, tiled=True
+        )
+        part = slab_rows // depth_count
+        own_rotation = lax.dynamic_slice_in_dim(rotation, layer_index * part, part, 0)
+        return series(rows_count, piece, own_rotation)
     mirrored = lax.all_to_all(local_sum, ("row", "col"), split_axis=1, concat_axis=0, tiled=True).T
     operator_rows = (
         lax.psum_scatter(local_sum - mirrored, "depth", scatter_dimension=1, tiled=True) * factor
@@ -79,6 +300,8 @@
         P(("row", "col"), None),
     )
     out_specs = P(("row", "col"), "depth")
+    rows_count = mesh.shape["row"]
+    fast = mesh.shape["col"] == 4 and mesh.shape["depth"] == 2
     return jax.shard_map(
-        per_device, mesh=mesh, in_specs=in_specs, out_specs=out_specs, check_vma=False
-    )
+        functools.partial(per_device, rows_count, fast), mesh=mesh, in_specs=in_specs, out_specs=out_specs, check_vma=False
+    )

time: 656 us -> 380 us (0.58); the launches traced: 647 us -> 380 us
  waiting for transfers between devices: 371 us -> 31.3 us
  Pallas kernels: 0 us -> 221 us
  matrix products: 85 us -> 0.82 us
  blocking collectives: 128 us -> 82.9 us
  starting transfers between devices: 10.1 us -> 0.01 us
  local copies, waits for them, and re-layouts: 24.7 us -> 18.1 us
    all_gather x7 -> x0, waiting for transfers between devices: 317 us -> none  [the longest x6 186 us: per_device(): piece = lax.all_gather(series_term, 'depth', axis=1, tiled=True)]
    pallas_call x0 -> x1, Pallas kernels: none -> 221 us  [series(): pl.pallas_call(functools.partial(series_kernel, rows_count), out_shape=ja...]
    dot_general x7 -> x0, matrix products: 84.8 us -> none  [the longest x6 75.6 us: per_device(): jnp.dot(piece, matching, preferred_element_type=jnp.float32)]
    all_to_all x1, blocking collectives: 96.2 us -> 50.9 us  [per_device(): lax.all_to_all(narrow, ('row', 'col'), split_axis=1, concat_axis=0, tiled...]
    reduce_scatter x1, waiting for transfers between devices: 53.8 us -> 31.2 us  [per_device(): lax.psum_scatter(anti.astype(jnp.bfloat16), 'depth', scatter_dimension=0,...]
    all_gather x7 -> x0, starting transfers between devices: 10.1 us -> none  [the longest x6 10.1 us: per_device(): piece = lax.all_gather(series_term, 'depth', axis=1, tiled=True)]
    mul x1 -> x0, other arithmetic: 8.24 us -> none  [per_device(): local_sum = jnp.sum(own_weights[:, None, None] * terms, 0)]
    convert_element_type x1 -> x2, other arithmetic: 2.77 us -> 9.47 us  [the longest x1 5.86 us: per_device(): narrow = local_sum.astype(jnp.bfloat16)]
  transfers between devices with their start and end apart: 8 -> 1, of which waited for: 8 -> 1; matrix products, arithmetic and copies ran while one was open for 0% -> 0% of each run, Pallas kernels for 0% -> 0%
where the time goes in v1:
time: 380 us
  Pallas kernels  221 us (58%)
  blocking collectives  82.9 us (22%)
  waiting for transfers between devices  31.3 us (8%)
  local copies, waits for them, and re-layouts  18.1 us (5%)
  between operations  14.2 us (4%)
  other arithmetic  11 us (3%)
    pallas_call x1, Pallas kernels, series(): pl.pallas_call(functools.partial(series_kernel, rows_count), out_shape=ja...  221 us
    all_to_all x1, blocking collectives, per_device(): lax.all_to_all(narrow, ('row', 'col'), split_axis=1, concat_axis=0, tiled...  50.9 us
    reduce_scatter x1, waiting for transfers between devices, per_device(): lax.psum_scatter(anti.astype(jnp.bfloat16), 'depth', scatter_dimension=0,...  31.2 us
    all_gather x1, blocking collectives, per_device(): lax.all_gather(diag_piece, ('row', 'col'), axis=2, tiled=True)  23.1 us
    psum x1, blocking collectives, per_device(): centre = lax.psum(partial_centre, 'depth')  8.9 us
  transfers between devices with their start and end apart: 1, of which 1 were waited for; matrix products, arithmetic and copies ran while one was open for 0% of the time, Pallas kernels for 0%

profile of v1, /device:TPU:0, one launch (start us, length us, event | category | flops | bytes accessed | tf_op | source)
XLA Modules:
  0.0 379.6 jit_solution(14148455660998956862)
XLA Ops:
  6.5 0.0 copy-start
  6.5 0.0 reduce-scatter.2.cloned.1.call-start
  6.6 1.1 dynamic-slice_bitcast_fusion
  7.7 2.5 gather_fusion.1
  10.2 2.5 gather_fusion
  12.7 23.1 %all_gather.3 = bf16[1,2,4096]{2,1,0:T(2,128)(2,1)S(1)} all-gather(bf16[1,2,256]{2,1,0:T(2,128)(2,1)S(1)} %pad_maximum_fusion), channel_id=1, replica_groups=mesh['row'=4,'col'=4,'depth'=2] {'row','col'}, dimensions={2}, use_global_device_ids=true | all-gather | bytes 17408 | tf_op jit(solution)/shard_map/all_gather | solution.py:242
  35.9 0.2 slice_atan2_fusion
  36.1 1.3 dynamic_slice.15
  38.0 0.7 multiply_bitcast_fusion
  38.7 0.1 multiply_negate_fusion
  38.8 8.9 %psum.7 = bf16[3,4096]{1,0:T(4,128)(2,1)S(1)} all-reduce(f32[3,4096]{1,0:T(4,128)S(1)} %multiply_negate_fusion), channel_id=1, replica_groups=mesh['row'=4,'col'=4,'depth'=2] {'depth'}, use_global_device_ids=true, to_apply=%region_0.1 | all-reduce | flops 12288 | bytes 73728 | tf_op jit(solution)/shard_map/psum | solution.py:247
  47.7 0.8 fusion.9
  48.5 5.9 %fusion.15 = bf16[1,256,4096]{2,1,0:T(8,128)(2,1)} fusion(f32[4096]{0:T(1024)S(1)} %bitcast.41, f32[4096]{0:T(1024)S(1)} %atan2_add_fusion, f32[4096]{0:T(1024)S(1)} %bitcast.39, bf16[1,256,4096]{2,1,0:T(8,128)(2,1)} %param.6, f32[4096]{0:T(1024)S(1)} %bitcast.36, bf16[1,256,4096]{2,1,0:T(8,128)(2,1)} %param.5, f32[]{:T(128)} %bitcast), kind=kLoop, calls=%fused_computation.33 | loop fusion | flops 13631488 | bytes 6356996 | tf_op jit(solution)/shard_map/convert_element_type | solution.py:263
  54.4 4.1 %copy.10 = bf16[1,256,4096]{1,2,0:T(8,128)(2,1)} copy(bf16[1,256,4096]{2,1,0:T(8,128)(2,1)} %fusion.15) | data formatting | bytes 4194304 | tf_op jit(solution)/shard_map/convert_element_type | solution.py:263
  58.5 50.9 %all_to_all.10 = bf16[256,16,256]{0,2,1:T(8,128)(2,1)S(1)} all-to-all(bf16[256,16,256]{0,2,1:T(8,128)(2,1)} %bitcast.34), channel_id=1, replica_groups=mesh['row'=4,'col'=4,'depth'=2] {'row','col'}, dimensions={1} | all-to-all | bytes 4194304 | tf_op jit(solution)/shard_map/all_to_all | solution.py:264
  109.4 0.4 convert_bitcast_fusion
  109.9 0.0 copy-start.2
  109.9 0.0 copy-start.3
  109.9 0.5 copy.11
  110.4 1.0 copy-done.2
  111.5 0.6 copy-done.3
  112.1 3.6 fusion.7
  115.7 0.0 reduce-scatter.2.cloned.1.call-update
  115.7 0.0 copy-done
  115.7 0.1 constant_dynamic-slice_fusion.rotation_ref
  115.8 31.2 %reduce-scatter.2.cloned.1.call-done.piece_ref = bf16[128,4096]{1,0:T(8,128)(2,1)} async-done(((bf16[256,4096]{1,0:T(8,128)(2,1)}), bf16[128,4096]{1,0:T(8,128)(2,1)}) %reduce-scatter.2.cloned.1.call-update) | async-done | bytes 1048592 | tf_op jit(solution)/shard_map/reduce_scatter | solution.py:266
  147.1 0.0 copy-start.1
  147.1 1.2 copy-done.1
  148.3 221.4 %shard_map.55 = f32[256,2048]{1,0:T(8,128)} custom-call(bf16[128,4096]{1,0:T(8,128)(2,1)S(1)} %copy-done.1, bf16[128,4096]{1,0:T(8,128)(2,1)S(1)} %constant_dynamic-slice_fusion.rotation_ref), custom_call_target="tpu_custom_call" | custom-call | tf_op jit(solution)/shard_map/pallas_call | solution.py:201
  369.7 3.1 copy.13
  (7 shorter events, 0.1 us)
Async XLA Ops:
  6.5 109.2 %copy-start = (bf16[256,4096]{1,0:T(8,128)(2,1)S(1)}, bf16[256,4096]{1,0:T(8,128)(2,1)}, u32[]{:S(2)}) copy-start(bf16[256,4096]{1,0:T(8,128)(2,1)} %param.9) | copy-start | bytes 6291460
  6.5 140.5 %reduce-scatter.2.cloned.1.call-start = ((), (), s32[]{:S(2)}) async-start(), calls=%async_computation.2 | async-start | bytes 3145728 | tf_op jit(solution)/shard_map/reduce_scatter | solution.py:266
  109.9 1.6 copy-start.2
  109.9 2.2 copy-start.3
  147.1 1.2 copy-start.1
Sparse Core Ops, SparseCore 0:
  115.8 31.1 reduce-scatter.1

commit v2 on v1

--- a/solution.py
+++ b/solution.py
@@ -239,13 +239,28 @@
     own_vectors = (
         lax.dynamic_slice_in_dim(shells, first_shell, shells_here, 0).astype(jnp.float32) * LATTICE
     )
-    diagonals = lax.all_gather(diag_piece, ("row", "col"), axis=2, tiled=True).astype(jnp.float32)
-    diag_re = diagonals[:, 0]
-    diag_im = diagonals[:, 1]
-    phase_own = jnp.arctan2(diag_im, diag_re)
-    partial_centre = -jnp.einsum("bk,bn->kn", own_weights[:, None] * own_vectors, phase_own)
-    centre = lax.psum(partial_centre, "depth")
-    spread = phase_own + jnp.einsum("bk,kn->bn", own_vectors, centre)
+    if fast:
+        every = lax.all_gather(diag_piece, ("row", "col", "depth"), axis=0, tiled=False)
+        every = every.reshape(-1, depth_count, shells_here, 2, slab_rows)
+        every = every.transpose(1, 2, 3, 0, 4).reshape(depth_count * shells_here, 2, width)
+        every = every.astype(jnp.float32)
+        phases = jnp.arctan2(every[:, 1], every[:, 0])
+        vectors = shells.astype(jnp.float32) * LATTICE
+        scaled = weights[:, None] * vectors
+        centre = -jnp.sum(scaled[:, :, None] * phases[:, None, :], 0)
+        own_diag = lax.dynamic_slice_in_dim(every, first_shell, shells_here, 0)
+        diag_re = own_diag[:, 0]
+        diag_im = own_diag[:, 1]
+        phase_own = lax.dynamic_slice_in_dim(phases, first_shell, shells_here, 0)
+        spread = phase_own + jnp.sum(own_vectors[:, :, None] * centre[None], 1)
+    else:
+        diagonals = lax.all_gather(diag_piece, ("row", "col"), axis=2, tiled=True).astype(jnp.float32)
+        diag_re = diagonals[:, 0]
+        diag_im = diagonals[:, 1]
+        phase_own = jnp.arctan2(diag_im, diag_re)
+        partial_centre = -jnp.einsum("bk,bn->kn", own_weights[:, None] * own_vectors, phase_own)
+        centre = lax.psum(partial_centre, "depth")
+        spread = phase_own + jnp.einsum("bk,kn->bn", own_vectors, centre)
     modulus = diag_re * diag_re + diag_im * diag_im
     values_re = intersection_re.astype(jnp.float32)
     values_im = intersection_im.astype(jnp.float32)
@@ -260,12 +275,14 @@
     factor = 1.25 / math.sqrt(depth_count * shells_here)
     slab_cols = width // depth_count
     if fast:
-        narrow = local_sum.astype(jnp.bfloat16)
-        mirrored = lax.all_to_all(narrow, ("row", "col"), split_axis=1, concat_axis=0, tiled=True)
-        anti = (local_sum - mirrored.T.astype(jnp.float32)) * factor
-        piece = lax.psum_scatter(
-            anti.astype(jnp.bfloat16), "depth", scatter_dimension=0, tiled=True
+        summed = lax.psum_scatter(
+            local_sum.astype(jnp.bfloat16), "depth", scatter_dimension=0, tiled=True
         )
+        mirrored = lax.all_to_all(
+            summed, ("row", "col", "depth"), split_axis=1, concat_axis=0, tiled=True
+        )
+        anti = (summed.astype(jnp.float32) - mirrored.T.astype(jnp.float32)) * factor
+        piece = anti.astype(jnp.bfloat16)
         part = slab_rows // depth_count
         own_rotation = lax.dynamic_slice_in_dim(rotation, layer_index * part, part, 0)
         return series(rows_count, piece, own_rotation)

time: 380 us -> 386 us (1.016)
  waiting for transfers between devices: 31.3 us -> 54 us
  blocking collectives: 82.9 us -> 69.7 us
  local copies, waits for them, and re-layouts: 18.1 us -> 12.8 us
  starting transfers between devices: 0.01 us -> 4.73 us
    all_to_all x1 -> x0, blocking collectives: 50.9 us -> none  [per_device(): lax.all_to_all(narrow, ('row', 'col'), split_axis=1, concat_axis=0, tiled...]
    all_gather x1, blocking collectives: 23.1 us -> 69.7 us  [per_device(): lax.all_gather(diag_piece, ('row', 'col', 'depth'), axis=0, tiled=False)]
    all_to_all x0 -> x1, waiting for transfers between devices: none -> 26.1 us  [per_device(): lax.all_to_all(summed, ('row', 'col', 'depth'), split_axis=1, concat_axis...]
    psum x1 -> x0, blocking collectives: 8.9 us -> none  [per_device(): centre = lax.psum(partial_centre, 'depth')]
    all_to_all x0 -> x1, starting transfers between devices: none -> 4.73 us  [per_device(): lax.all_to_all(summed, ('row', 'col', 'depth'), split_axis=1, concat_axis...]
    convert_element_type x2, local copies, waits for them, and re-layouts: 4.6 us -> 0.06 us  [per_device(): every = every.astype(jnp.float32)]
  transfers between devices with their start and end apart: 1 -> 2, of which waited for: 1 -> 2; matrix products, arithmetic and copies ran while one was open for 0% -> 0% of each run, Pallas kernels for 0% -> 0%
where the time goes in v2:
time: 386 us
  Pallas kernels  223 us (58%)
  blocking collectives  69.7 us (18%)
  waiting for transfers between devices  54 us (14%)
  between operations  13.6 us (4%)
  local copies, waits for them, and re-layouts  12.8 us (3%)
  other arithmetic  8.22 us (2%)
  starting transfers between devices  4.73 us (1%)
    pallas_call x1, Pallas kernels, series(): pl.pallas_call(functools.partial(series_kernel, rows_count), out_shape=ja...  223 us
    all_gather x1, blocking collectives, per_device(): lax.all_gather(diag_piece, ('row', 'col', 'depth'), axis=0, tiled=False)  69.7 us
    reduce_scatter x1, waiting for transfers between devices, per_device(): lax.psum_scatter(local_sum.astype(jnp.bfloat16), 'depth', scatter_dimensi...  27.9 us
    all_to_all x1, waiting for transfers between devices, per_device(): lax.all_to_all(summed, ('row', 'col', 'depth'), split_axis=1, concat_axis...  26.1 us
  transfers between devices with their start and end apart: 2, of which 2 were waited for; matrix products, arithmetic and copies ran while one was open for 0% of the time, Pallas kernels for 0%

profile of v2, /device:TPU:0, one launch (start us, length us, event | category | flops | bytes accessed | tf_op | source)
XLA Modules:
  0.0 385.7 jit_solution(10848233336910981688)
XLA Ops:
  6.5 0.0 copy-start
  6.5 0.0 copy-start.2
  6.5 0.0 copy-start.1
  6.5 0.0 reduce-scatter.2.cloned.1.call-start
  6.6 1.1 dynamic-slice_bitcast_fusion
  7.7 2.5 gather_fusion.1
  10.2 2.5 gather_fusion
  12.7 69.7 %all-gather = bf16[32,2,256]{2,1,0:T(2,128)(2,1)S(1)} all-gather(bf16[1,2,256]{2,1,0:T(2,128)(2,1)S(1)} %pad_maximum_fusion), channel_id=2, replica_groups=mesh['row'=4,'col'=4,'depth'=2] {'row','col','depth'}, dimensions={0}, use_global_device_ids=true | all-gather | bytes 33792 | tf_op jit(solution)/shard_map/all_gather | solution.py:243
  82.6 0.4 slice_atan2_fusion
  83.0 0.0 copy-done.2
  83.1 0.6 dynamic_slice.23
  83.7 0.0 copy-done.1
  83.7 0.1 convert_multiply_fusion.4
  83.8 0.1 copy.14
  83.8 0.2 multiply_reduce_fusion
  84.1 0.1 fusion.11
  84.2 5.9 %fusion.10 = bf16[256,4096]{1,0:T(8,128)(2,1)} fusion(f32[4096]{0:T(1024)S(1)} %bitcast.58, f32[4096]{0:T(1024)S(1)} %bitcast.57, f32[4096]{0:T(1024)S(1)} %bitcast.60, bf16[1,256,4096]{2,1,0:T(8,128)(2,1)} %param.6, f32[4096]{0:T(1024)S(1)} %bitcast.59, bf16[1,256,4096]{2,1,0:T(8,128)(2,1)} %param.5, f32[]{:T(128)} %bitcast), kind=kLoop, calls=%fused_computation.18 | loop fusion | flops 13631488 | bytes 6356996 | tf_op jit(solution)/shard_map/convert_element_type | solution.py:279
  90.1 0.0 reduce-scatter.2.cloned.1.call-update
  90.1 27.9 %reduce-scatter.2.cloned.1.call-done = bf16[128,4096]{1,0:T(8,128)(2,1)} async-done(((bf16[256,4096]{1,0:T(8,128)(2,1)}), bf16[128,4096]{1,0:T(8,128)(2,1)}) %reduce-scatter.2.cloned.1.call-update) | async-done | bytes 1048592 | tf_op jit(solution)/shard_map/reduce_scatter | solution.py:278
  118.0 2.3 copy.18
  120.3 4.7 %all-to-all-start = ((bf16[128,32,128]{0,2,1:T(8,128)(2,1)}), bf16[128,32,128]{0,2,1:T(8,128)(2,1)}, u32[]{:S(2)}, u32[]{:S(2)}) async-start(bf16[128,32,128]{0,2,1:T(8,128)(2,1)} %bitcast.15), calls=%async_computation.1 | async-start | bytes 2097152 | tf_op jit(solution)/shard_map/all_to_all | solution.py:281
  125.0 0.0 copy-done
  125.0 0.1 constant_dynamic-slice_fusion.1.rotation_ref
  125.1 26.1 %all-to-all-done = bf16[128,32,128]{0,2,1:T(8,128)(2,1)} async-done(((bf16[128,32,128]{0,2,1:T(8,128)(2,1)}), bf16[128,32,128]{0,2,1:T(8,128)(2,1)}, u32[]{:S(2)}, u32[]{:S(2)}) %all-to-all-start) | async-done | bytes 1048608 | tf_op jit(solution)/shard_map/all_to_all | solution.py:281
  151.2 1.8 fusion.9.piece_ref
  153.1 222.7 %shard_map.55 = f32[256,2048]{1,0:T(8,128)} custom-call(bf16[128,4096]{1,0:T(8,128)(2,1)S(1)} %fusion.9.piece_ref, bf16[128,4096]{1,0:T(8,128)(2,1)S(1)} %constant_dynamic-slice_fusion.1.rotation_ref), custom_call_target="tpu_custom_call" | custom-call | tf_op jit(solution)/shard_map/pallas_call | solution.py:201
  375.7 3.1 copy.26
  (12 shorter events, 0.2 us)
Async XLA Ops:
  6.5 118.5 %copy-start = (bf16[256,4096]{1,0:T(8,128)(2,1)S(1)}, bf16[256,4096]{1,0:T(8,128)(2,1)}, u32[]{:S(2)}) copy-start(bf16[256,4096]{1,0:T(8,128)(2,1)} %param.9) | copy-start | bytes 6291460
  6.5 76.5 %copy-start.2 = (f32[2]{0:T(128)S(1)}, f32[2]{0:T(128)}, u32[]{:S(2)}) copy-start(f32[2]{0:T(128)} %param.7) | copy-start | bytes 28
  6.5 77.1 %copy-start.1 = (s32[2,3]{1,0:T(2,128)S(1)}, s32[2,3]{1,0:T(2,128)}, u32[]{:S(2)}) copy-start(s32[2,3]{1,0:T(2,128)} %param.8) | copy-start | bytes 76
  6.5 111.5 %reduce-scatter.2.cloned.1.call-start = ((), (), s32[]{:S(2)}) async-start(), calls=%async_computation.2 | async-start | bytes 3145728 | tf_op jit(solution)/shard_map/reduce_scatter | solution.py:278
  120.3 30.9 %all-to-all-start = ((bf16[128,32,128]{0,2,1:T(8,128)(2,1)}), bf16[128,32,128]{0,2,1:T(8,128)(2,1)}, u32[]{:S(2)}, u32[]{:S(2)}) async-start(bf16[128,32,128]{0,2,1:T(8,128)(2,1)} %bitcast.15), calls=%async_computation.1 | async-start | bytes 2097152 | tf_op jit(solution)/shard_map/all_to_all | solution.py:281
Sparse Core Ops, SparseCore 0:
  90.3 27.6 reduce-scatter.1

commit v3 on v1

--- a/solution.py
+++ b/solution.py
@@ -260,12 +260,14 @@
     factor = 1.25 / math.sqrt(depth_count * shells_here)
     slab_cols = width // depth_count
     if fast:
-        narrow = local_sum.astype(jnp.bfloat16)
-        mirrored = lax.all_to_all(narrow, ("row", "col"), split_axis=1, concat_axis=0, tiled=True)
-        anti = (local_sum - mirrored.T.astype(jnp.float32)) * factor
-        piece = lax.psum_scatter(
-            anti.astype(jnp.bfloat16), "depth", scatter_dimension=0, tiled=True
+        summed = lax.psum_scatter(
+            local_sum.astype(jnp.bfloat16), "depth", scatter_dimension=0, tiled=True
         )
+        mirrored = lax.all_to_all(
+            summed, ("row", "col", "depth"), split_axis=1, concat_axis=0, tiled=True
+        )
+        anti = (summed.astype(jnp.float32) - mirrored.T.astype(jnp.float32)) * factor
+        piece = anti.astype(jnp.bfloat16)
         part = slab_rows // depth_count
         own_rotation = lax.dynamic_slice_in_dim(rotation, layer_index * part, part, 0)
         return series(rows_count, piece, own_rotation)

time: 380 us -> 350 us (0.921)
  blocking collectives: 82.9 us -> 32 us
  waiting for transfers between devices: 31.3 us -> 54.4 us
  local copies, waits for them, and re-layouts: 18.1 us -> 12.9 us
  starting transfers between devices: 0.01 us -> 4.75 us
    all_to_all x1 -> x0, blocking collectives: 50.9 us -> none  [per_device(): lax.all_to_all(narrow, ('row', 'col'), split_axis=1, concat_axis=0, tiled...]
    all_to_all x0 -> x1, waiting for transfers between devices: none -> 26.1 us  [per_device(): lax.all_to_all(summed, ('row', 'col', 'depth'), split_axis=1, concat_axis...]
    all_to_all x0 -> x1, starting transfers between devices: none -> 4.75 us  [per_device(): lax.all_to_all(summed, ('row', 'col', 'depth'), split_axis=1, concat_axis...]
    convert_element_type x2 -> x0, local copies, waits for them, and re-layouts: 4.6 us -> none  [the longest x1 4.06 us: per_device(): narrow = local_sum.astype(jnp.bfloat16)]
  transfers between devices with their start and end apart: 1 -> 2, of which waited for: 1 -> 2; matrix products, arithmetic and copies ran while one was open for 0% -> 0% of each run, Pallas kernels for 0% -> 0%
where the time goes in v3:
time: 350 us
  Pallas kernels  223 us (64%)
  waiting for transfers between devices  54.4 us (16%)
  blocking collectives  32 us (9%)
  between operations  14.1 us (4%)
  local copies, waits for them, and re-layouts  12.9 us (4%)
  other arithmetic  8.79 us (3%)
  starting transfers between devices  4.75 us (1%)
    pallas_call x1, Pallas kernels, series(): pl.pallas_call(functools.partial(series_kernel, rows_count), out_shape=ja...  223 us
    reduce_scatter x1, waiting for transfers between devices, per_device(): lax.psum_scatter(local_sum.astype(jnp.bfloat16), 'depth', scatter_dimensi...  28.2 us
    all_to_all x1, waiting for transfers between devices, per_device(): lax.all_to_all(summed, ('row', 'col', 'depth'), split_axis=1, concat_axis...  26.1 us
    all_gather x1, blocking collectives, per_device(): lax.all_gather(diag_piece, ('row', 'col'), axis=2, tiled=True)  23.1 us
    psum x1, blocking collectives, per_device(): centre = lax.psum(partial_centre, 'depth')  8.9 us
  transfers between devices with their start and end apart: 2, of which 2 were waited for; matrix products, arithmetic and copies ran while one was open for 0% of the time, Pallas kernels for 0%

profile of v3, /device:TPU:0, one launch (start us, length us, event | category | flops | bytes accessed | tf_op | source)
XLA Modules:
  0.0 349.7 jit_solution(7744337723839785169)
XLA Ops:
  6.5 0.0 copy-start
  6.5 0.0 copy-start.1
  6.5 0.0 reduce-scatter.2.cloned.1.call-start
  6.6 1.1 dynamic-slice_bitcast_fusion
  7.7 2.5 gather_fusion.1
  10.2 2.5 gather_fusion
  12.7 23.1 %all_gather.3 = bf16[1,2,4096]{2,1,0:T(2,128)(2,1)S(1)} all-gather(bf16[1,2,256]{2,1,0:T(2,128)(2,1)S(1)} %pad_maximum_fusion), channel_id=1, replica_groups=mesh['row'=4,'col'=4,'depth'=2] {'row','col'}, dimensions={2}, use_global_device_ids=true | all-gather | bytes 17408 | tf_op jit(solution)/shard_map/all_gather | solution.py:242
  35.9 0.2 slice_atan2_fusion
  36.1 1.3 dynamic_slice.15
  38.0 0.7 multiply_bitcast_fusion
  38.7 0.1 multiply_negate_fusion
  38.8 8.9 %psum.7 = bf16[3,4096]{1,0:T(4,128)(2,1)S(1)} all-reduce(f32[3,4096]{1,0:T(4,128)S(1)} %multiply_negate_fusion), channel_id=1, replica_groups=mesh['row'=4,'col'=4,'depth'=2] {'depth'}, use_global_device_ids=true, to_apply=%region_0.1 | all-reduce | flops 12288 | bytes 73728 | tf_op jit(solution)/shard_map/psum | solution.py:247
  47.7 0.0 copy-done.1
  47.7 0.1 fusion.12
  47.9 5.9 %fusion.10 = bf16[256,4096]{1,0:T(8,128)(2,1)} fusion(f32[4096]{0:T(1024)S(1)} %bitcast.47, f32[4096]{0:T(1024)S(1)} %atan2_add_fusion, f32[4096]{0:T(1024)S(1)} %bitcast.46, bf16[1,256,4096]{2,1,0:T(8,128)(2,1)} %param.6, f32[4096]{0:T(1024)S(1)} %bitcast.44, bf16[1,256,4096]{2,1,0:T(8,128)(2,1)} %param.5, f32[]{:T(128)} %bitcast), kind=kLoop, calls=%fused_computation.18 | loop fusion | flops 13631488 | bytes 6356996 | tf_op jit(solution)/shard_map/convert_element_type | solution.py:264
  53.7 0.0 reduce-scatter.2.cloned.1.call-update
  53.7 28.2 %reduce-scatter.2.cloned.1.call-done = bf16[128,4096]{1,0:T(8,128)(2,1)} async-done(((bf16[256,4096]{1,0:T(8,128)(2,1)}), bf16[128,4096]{1,0:T(8,128)(2,1)}) %reduce-scatter.2.cloned.1.call-update) | async-done | bytes 1048592 | tf_op jit(solution)/shard_map/reduce_scatter | solution.py:263
  82.0 2.3 copy.10
  84.3 4.7 %all-to-all-start = ((bf16[128,32,128]{0,2,1:T(8,128)(2,1)}), bf16[128,32,128]{0,2,1:T(8,128)(2,1)}, u32[]{:S(2)}, u32[]{:S(2)}) async-start(bf16[128,32,128]{0,2,1:T(8,128)(2,1)} %bitcast.13), calls=%async_computation.1 | async-start | bytes 2097152 | tf_op jit(solution)/shard_map/all_to_all | solution.py:266
  89.0 0.0 copy-done
  89.0 0.1 constant_dynamic-slice_fusion.rotation_ref
  89.1 26.1 %all-to-all-done = bf16[128,32,128]{0,2,1:T(8,128)(2,1)} async-done(((bf16[128,32,128]{0,2,1:T(8,128)(2,1)}), bf16[128,32,128]{0,2,1:T(8,128)(2,1)}, u32[]{:S(2)}, u32[]{:S(2)}) %all-to-all-start) | async-done | bytes 1048608 | tf_op jit(solution)/shard_map/all_to_all | solution.py:266
  115.2 1.8 fusion.9.piece_ref
  117.1 222.6 %shard_map.55 = f32[256,2048]{1,0:T(8,128)} custom-call(bf16[128,4096]{1,0:T(8,128)(2,1)S(1)} %fusion.9.piece_ref, bf16[128,4096]{1,0:T(8,128)(2,1)S(1)} %constant_dynamic-slice_fusion.rotation_ref), custom_call_target="tpu_custom_call" | custom-call | tf_op jit(solution)/shard_map/pallas_call | solution.py:201
  339.7 3.1 copy.14
  (7 shorter events, 0.1 us)
Async XLA Ops:
  6.5 82.5 %copy-start = (bf16[256,4096]{1,0:T(8,128)(2,1)S(1)}, bf16[256,4096]{1,0:T(8,128)(2,1)}, u32[]{:S(2)}) copy-start(bf16[256,4096]{1,0:T(8,128)(2,1)} %param.9) | copy-start | bytes 6291460
  6.5 41.1 %copy-start.1 = (s32[2,3]{1,0:T(2,128)S(1)}, s32[2,3]{1,0:T(2,128)}, u32[]{:S(2)}) copy-start(s32[2,3]{1,0:T(2,128)} %param.8) | copy-start | bytes 76
  6.5 75.5 %reduce-scatter.2.cloned.1.call-start = ((), (), s32[]{:S(2)}) async-start(), calls=%async_computation.2 | async-start | bytes 3145728 | tf_op jit(solution)/shard_map/reduce_scatter | solution.py:263
  84.3 31.0 %all-to-all-start = ((bf16[128,32,128]{0,2,1:T(8,128)(2,1)}), bf16[128,32,128]{0,2,1:T(8,128)(2,1)}, u32[]{:S(2)}, u32[]{:S(2)}) async-start(bf16[128,32,128]{0,2,1:T(8,128)(2,1)} %bitcast.13), calls=%async_computation.1 | async-start | bytes 2097152 | tf_op jit(solution)/shard_map/all_to_all | solution.py:266
Sparse Core Ops, SparseCore 0:
  53.9 28.0 reduce-scatter.1
